TPU v7x, 32 devices: a whole 2x2x4 slice. The times are simulated.
32 devices in a mesh: section: 4 (over x, core), expert: 8 (over z, y).
Axes of the slice: x: 2, y: 2, z: 4, core: 2. Of those that a mesh axis runs over, the one named last changes fastest.
Arguments:
- inputs: bfloat16 [4, 256, 2048], P(None, 'expert'), may hold values from -6 to 6
- cotangent: bfloat16 [4, 256, 2048], P(None, 'expert'), may hold values from -6 to 6
- norm_gain: bfloat16 [4, 2048], P('section'), may hold values from 0.25 to 1.75
- w_gate: bfloat16 [4, 8, 2048, 768], P('section', 'expert'), may hold values from -0.125 to 0.125
- w_up: bfloat16 [4, 8, 2048, 768], P('section', 'expert'), may hold values from -0.125 to 0.125
- w_down: bfloat16 [4, 8, 768, 2048], P('section', 'expert'), may hold values from -0.21875 to 0.21875
- route_ids: int32 [4, 4, 256, 2], P('section', None, 'expert'), may hold values from 0 to 7, all different within a row; in each aligned block of 32 rows (0 to 31, 32 to 63, ..., all dimensions but the last counted through in order) at most 16 rows name the same one
- route_weights: float32 [4, 4, 256, 2], P('section', None, 'expert'), may hold values from 0.2 to 1
Outputs:
- layer_outputs: bfloat16 [4, 4, 256, 2048], P('section', None, 'expert')
- input_grads: bfloat16 [4, 4, 256, 2048], P('section', None, 'expert')
Inputs may be any that keep to these rules, and one draw needn't show every extreme that they name: `route_ids`: each token names 2 different experts. In each aligned block of 32 rows (one device's tokens of one micro-batch in one layer) no expert is named by more than 16 tokens, and in some blocks an expert is named by exactly 16.
All inputs are finite; a program needn't handle non-finite values.
Results may differ from a plain program's by a relative error of at most 0.04.
Values may be sent and summed in bfloat16 or wider, within the bound.
A program may use at most 64 MiB of HBM per device.

v0:
```python
import jax
import jax.numpy as jnp
from jax import lax
from jax.sharding import PartitionSpec as P

EPS = 1e-06


def passed_along(shard, axis, by):
    size = lax.axis_size(axis)
    pairs = [(i, i + by) for i in range(size) if 0 <= i + by < size]
    return lax.ppermute(shard, axis, pairs)


def norm_forward(act, gain):
    values = act.astype(jnp.float32)
    scale = lax.rsqrt(jnp.mean(values * values, axis=-1, keepdims=True) + EPS)
    normed = (values * scale * gain.astype(jnp.float32)).astype(jnp.bfloat16)
    return (values, scale, normed)


def norm_backward(d_normed, values, scale, gain, upstream):
    scaled = d_normed * gain.astype(jnp.float32)
    inner = jnp.mean(scaled * values, axis=-1, keepdims=True)
    return (
        upstream.astype(jnp.float32) + scale * scaled - values * scale * scale * scale * inner
    ).astype(jnp.bfloat16)


def contract_last(left, right):
    return lax.dot_general(
        left, right, (((1,), (1,)), ((), ())), preferred_element_type=jnp.float32
    )


def contract_first(left, right, exact):
    if exact:
        return lax.dot_general(
            left,
            right,
            (((0,), (0,)), ((), ())),
            preferred_element_type=jnp.float32,
            precision=lax.Precision.HIGHEST,
        )
    return lax.dot_general(
        left, right, (((0,), (0,)), ((), ())), preferred_element_type=jnp.float32
    )


def expert_forward(rows, gate_w, up_w, down_w):
    gate = jnp.dot(rows, gate_w, preferred_element_type=jnp.float32)
    up = jnp.dot(rows, up_w, preferred_element_type=jnp.float32)
    hidden = (jax.nn.silu(gate) * up).astype(jnp.bfloat16)
    out = jnp.dot(hidden, down_w, preferred_element_type=jnp.float32).astype(jnp.bfloat16)
    return (out, gate, up)


def expert_backward(grads, gate, up, gate_w, up_w, down_w):
    d_hidden = contract_last(grads, down_w)
    sig = jax.nn.sigmoid(gate)
    d_gate = (d_hidden * up * sig * (1.0 + gate * (1.0 - sig))).astype(jnp.bfloat16)
    d_up = (d_hidden * gate * sig).astype(jnp.bfloat16)
    return (contract_last(d_gate, gate_w) + contract_last(d_up, up_w)).astype(jnp.bfloat16)


def route_tables(ids, weights, experts, capacity):
    micro, rows, top = ids.shape
    flat = ids.reshape(micro, rows * top)
    picks = (flat[:, :, None] == jnp.arange(experts, dtype=jnp.int32)[None, None, :]).astype(
        jnp.int32
    )
    earlier = jnp.cumsum(picks, axis=1) - picks
    slot = jnp.sum(earlier * picks, axis=2)
    target = flat * capacity + slot
    columns = jnp.arange(experts * capacity, dtype=jnp.int32)
    onehot = (target[:, :, None] == columns[None, None, :]).astype(jnp.float32)
    onehot = onehot.reshape(micro, rows, top, experts * capacity)
    dispatch = jnp.swapaxes(jnp.sum(onehot, axis=2), 1, 2).astype(jnp.bfloat16)
    combine = jnp.sum(onehot * weights[:, :, :, None], axis=2)
    return (dispatch, combine)


def shards(inputs, cotangent, norm_gain, w_gate, w_up, w_down, route_ids, route_weights):
    sections = lax.axis_size("section")
    section = lax.axis_index("section")
    experts = lax.axis_size("expert")
    micro, rows, width = inputs.shape
    top = route_ids.shape[3]
    hid = w_gate.shape[3]
    capacity = 2 * rows * top // experts
    slots = experts * capacity
    gain = norm_gain[0]
    gate_w = w_gate[0, 0]
    up_w = w_up[0, 0]
    down_w = w_down[0, 0]
    dispatch, combine = route_tables(route_ids[0], route_weights[0], experts, capacity)

    def forward_layer(act, index, active):
        values, scale, normed = norm_forward(act, gain)
        pick = lax.dynamic_index_in_dim(dispatch, index, 0, keepdims=False)
        mix = lax.dynamic_index_in_dim(combine, index, 0, keepdims=False)
        sending = jnp.dot(pick, normed, preferred_element_type=jnp.float32).astype(jnp.bfloat16)
        received = lax.all_to_all(
            sending.reshape(experts, capacity, width),
            "expert",
            split_axis=0,
            concat_axis=0,
            tiled=True,
        )
        sources, count, dim = received.shape
        flat_rows = received.reshape(sources * count, dim)

        def serve_working(block):
            return expert_forward(block, gate_w, up_w, down_w)

        def serve_resting(block):
            return (
                jnp.zeros_like(block),
                jnp.zeros((block.shape[0], hid), jnp.float32),
                jnp.zeros((block.shape[0], hid), jnp.float32),
            )

        out, gate, up = lax.cond(active, serve_working, serve_resting, flat_rows)
        back = lax.all_to_all(
            out.reshape(sources, count, dim), "expert", split_axis=0, concat_axis=0, tiled=True
        )
        back, gate, up = (back, gate.reshape(sources, count, hid), up.reshape(sources, count, hid))
        branch = jnp.dot(
            mix,
            back.reshape(slots, width).astype(jnp.float32),
            preferred_element_type=jnp.float32,
            precision=lax.Precision.HIGHEST,
        )
        out = (values + branch).astype(jnp.bfloat16)
        return (out, gate.reshape(slots, hid), up.reshape(slots, hid))

    def backward_layer(upstream, act, index, gate, up, active):
        values, scale, normed = norm_forward(act, gain)
        pick = lax.dynamic_index_in_dim(dispatch, index, 0, keepdims=False)
        mix = lax.dynamic_index_in_dim(combine, index, 0, keepdims=False)
        grad_rows = contract_first(mix, upstream.astype(jnp.float32), True).astype(jnp.bfloat16)
        grad_rows = grad_rows.reshape(experts, capacity, width)
        received = lax.all_to_all(grad_rows, "expert", split_axis=0, concat_axis=0, tiled=True)

        def backward_working(block):
            return expert_backward(block, gate, up, gate_w, up_w, down_w)

        def backward_resting(block):
            return jnp.zeros_like(block)

        d_rows = lax.cond(
            active, backward_working, backward_resting, received.reshape(slots, width)
        )
        returned = lax.all_to_all(
            d_rows.reshape(experts, capacity, width),
            "expert",
            split_axis=0,
            concat_axis=0,
            tiled=True,
        )
        d_normed = contract_first(pick, returned.reshape(slots, width), False)
        return norm_backward(d_normed, values, scale, gain, upstream)

    def keep_row(store, value, index, active):
        old = lax.dynamic_index_in_dim(store, index, 0, keepdims=False)
        fresh = jnp.where(active, value, old)
        return lax.dynamic_update_index_in_dim(store, fresh, index, 0)

    def forward_tick(position, state):
        incoming, saved_in, outputs, gates, ups = state
        active = jnp.logical_and(position >= 0, position < micro)
        index = jnp.clip(position, 0, micro - 1)
        first = lax.dynamic_index_in_dim(inputs, index, 0, keepdims=False)
        act = jnp.where(section == 0, first, incoming)
        out, gate, up = forward_layer(act, index, active)
        saved_in = keep_row(saved_in, act, index, active)
        outputs = keep_row(outputs, out, index, active)
        gates = keep_row(gates, gate, index, active)
        ups = keep_row(ups, up, index, active)
        incoming = passed_along(out, "section", 1)
        return (incoming, saved_in, outputs, gates, ups)

    def backward_tick(position, state, saved):
        incoming, grads = state
        saved_in, gates, ups = saved
        active = jnp.logical_and(position >= 0, position < micro)
        index = jnp.clip(position, 0, micro - 1)
        last = lax.dynamic_index_in_dim(cotangent, index, 0, keepdims=False)
        upstream = jnp.where(section == sections - 1, last, incoming)
        act = lax.dynamic_index_in_dim(saved_in, index, 0, keepdims=False)
        gate = lax.dynamic_index_in_dim(gates, index, 0, keepdims=False)
        up = lax.dynamic_index_in_dim(ups, index, 0, keepdims=False)
        grad = backward_layer(upstream, act, index, gate, up, active)
        grads = keep_row(grads, grad, index, active)
        incoming = passed_along(grad, "section", -1)
        return (incoming, grads)

    zero_rows = jnp.zeros((rows, width), jnp.bfloat16)
    zero_store = jnp.zeros((micro, rows, width), jnp.bfloat16)
    zero_hidden = jnp.zeros((micro, slots, hid), jnp.float32)
    forward_state = (zero_rows, zero_store, zero_store, zero_hidden, zero_hidden)
    backward_state = (zero_rows, zero_store)

    def forward_step(step, state):
        return forward_tick(step - section, state)

    forward_state = lax.fori_loop(0, micro + sections - 1, forward_step, forward_state)
    saved = (forward_state[1], forward_state[3], forward_state[4])

    def backward_step(step, state):
        return backward_tick(step - (sections - 1 - section), state, saved)

    backward_state = lax.fori_loop(0, micro + sections - 1, backward_step, backward_state)
    layer_outputs = forward_state[2][None]
    input_grads = backward_state[1][None]
    return (layer_outputs, input_grads)


def solution(mesh):
    return jax.shard_map(
        shards,
        mesh=mesh,
        in_specs=(
            P(None, "expert", None),
            P(None, "expert", None),
            P("section", None),
            P("section", "expert", None, None),
            P("section", "expert", None, None),
            P("section", "expert", None, None),
            P("section", None, "expert", None),
            P("section", None, "expert", None),
        ),
        out_specs=(P("section", None, "expert", None), P("section", None, "expert", None)),
        check_vma=False,
    )
```

profile of v0, /device:TPU:0, one launch (start us, length us, event | category | flops | bytes accessed | tf_op | source)
XLA Modules:
  0.0 740.2 jit_solution(15604990136691543007)
XLA Ops:
  9.5 375.5 %while.39 = (s32[]{:T(128)}, bf16[32,2048]{1,0:T(8,128)(2,1)S(1)}, bf16[4,32,2048]{2,1,0:T(8,128)(2,1)}, bf16[4,32,2048]{2,1,0:T(8,128)(2,1)}, f32[4,128,768]{2,...) while((s32[]{:T(128)}, bf16[32,2048]{1,0:T(8,128)(2,1)S(1)}, ...), condition=%wide.region_8.9_spmd, body=%wide.region_4.8_spmd.sunk | while | flops 1327564800 | bytes 37952480 | solution.py:207
  21.4 14.6 %all-to-all-done = bf16[8,16,2048]{2,1,0:T(8,128)(2,1)} async-done(((bf16[8,16,2048]{2,1,0:T(8,128)(2,1)}), bf16[8,16,2048]{2,1,0:T(8,128)(2,1)}, u32[]{:S(2)}, u32[]{:S(2)}) %all-to-all-start) | async-done | bytes 524320 | tf_op jit(solution)/shard_map/while/body/eval_jaxpr/all_to_all | solution.py:103
  73.3 14.9 %all-to-all-done = bf16[8,16,2048]{2,1,0:T(8,128)(2,1)} async-done(((bf16[8,16,2048]{2,1,0:T(8,128)(2,1)}), bf16[8,16,2048]{2,1,0:T(8,128)(2,1)}, u32[]{:S(2)}, u32[]{:S(2)}) %all-to-all-start) | async-done | bytes 524320 | tf_op jit(solution)/shard_map/while/body/eval_jaxpr/all_to_all | solution.py:103
  129.6 14.6 %all-to-all-done = bf16[8,16,2048]{2,1,0:T(8,128)(2,1)} async-done(((bf16[8,16,2048]{2,1,0:T(8,128)(2,1)}), bf16[8,16,2048]{2,1,0:T(8,128)(2,1)}, u32[]{:S(2)}, u32[]{:S(2)}) %all-to-all-start) | async-done | bytes 524320 | tf_op jit(solution)/shard_map/while/body/eval_jaxpr/all_to_all | solution.py:103
  161.3 9.8 %all-to-all-done.1 = bf16[8,16,2048]{2,1,0:T(8,128)(2,1)} async-done(((bf16[8,16,2048]{2,1,0:T(8,128)(2,1)}), bf16[8,16,2048]{2,1,0:T(8,128)(2,1)}, u32[]{:S(2)}, u32[]{:S(2)}) %all-to-all-start.1) | async-done | bytes 524320 | tf_op jit(solution)/shard_map/while/body/eval_jaxpr/all_to_all | solution.py:124
  185.6 14.7 %all-to-all-done = bf16[8,16,2048]{2,1,0:T(8,128)(2,1)} async-done(((bf16[8,16,2048]{2,1,0:T(8,128)(2,1)}), bf16[8,16,2048]{2,1,0:T(8,128)(2,1)}, u32[]{:S(2)}, u32[]{:S(2)}) %all-to-all-start) | async-done | bytes 524320 | tf_op jit(solution)/shard_map/while/body/eval_jaxpr/all_to_all | solution.py:103
  217.4 9.8 %all-to-all-done.1 = bf16[8,16,2048]{2,1,0:T(8,128)(2,1)} async-done(((bf16[8,16,2048]{2,1,0:T(8,128)(2,1)}), bf16[8,16,2048]{2,1,0:T(8,128)(2,1)}, u32[]{:S(2)}, u32[]{:S(2)}) %all-to-all-start.1) | async-done | bytes 524320 | tf_op jit(solution)/shard_map/while/body/eval_jaxpr/all_to_all | solution.py:124
  241.7 14.7 %all-to-all-done = bf16[8,16,2048]{2,1,0:T(8,128)(2,1)} async-done(((bf16[8,16,2048]{2,1,0:T(8,128)(2,1)}), bf16[8,16,2048]{2,1,0:T(8,128)(2,1)}, u32[]{:S(2)}, u32[]{:S(2)}) %all-to-all-start) | async-done | bytes 524320 | tf_op jit(solution)/shard_map/while/body/eval_jaxpr/all_to_all | solution.py:103
  293.5 15.2 %all-to-all-done = bf16[8,16,2048]{2,1,0:T(8,128)(2,1)} async-done(((bf16[8,16,2048]{2,1,0:T(8,128)(2,1)}), bf16[8,16,2048]{2,1,0:T(8,128)(2,1)}, u32[]{:S(2)}, u32[]{:S(2)}) %all-to-all-start) | async-done | bytes 524320 | tf_op jit(solution)/shard_map/while/body/eval_jaxpr/all_to_all | solution.py:103
  319.7 9.9 %all-to-all-done.1 = bf16[8,16,2048]{2,1,0:T(8,128)(2,1)} async-done(((bf16[8,16,2048]{2,1,0:T(8,128)(2,1)}), bf16[8,16,2048]{2,1,0:T(8,128)(2,1)}, u32[]{:S(2)}, u32[]{:S(2)}) %all-to-all-start.1) | async-done | bytes 524320 | tf_op jit(solution)/shard_map/while/body/eval_jaxpr/all_to_all | solution.py:124
  343.8 14.9 %all-to-all-done = bf16[8,16,2048]{2,1,0:T(8,128)(2,1)} async-done(((bf16[8,16,2048]{2,1,0:T(8,128)(2,1)}), bf16[8,16,2048]{2,1,0:T(8,128)(2,1)}, u32[]{:S(2)}, u32[]{:S(2)}) %all-to-all-start) | async-done | bytes 524320 | tf_op jit(solution)/shard_map/while/body/eval_jaxpr/all_to_all | solution.py:103
  385.9 354.3 %while.40 = (s32[]{:T(128)}, bf16[32,2048]{1,0:T(8,128)(2,1)S(1)}, bf16[4,32,2048]{2,1,0:T(8,128)(2,1)}, pred[]{:T(512)}, s32[]{:T(128)}, /*index=5*/bf16[4,32,2...) while((s32[]{:T(128)}, bf16[32,2048]{1,0:T(8,128)(2,1)S(1)}, ...), condition=%wide.region_14.15_spmd, body=%wide.region_9.14_spmd.sunk | while | flops 1329006720 | bytes 40576464 | solution.py:213
  392.4 14.8 %all-to-all-done.2 = bf16[8,16,2048]{2,1,0:T(8,128)(2,1)} async-done(((bf16[8,16,2048]{2,1,0:T(8,128)(2,1)}), bf16[8,16,2048]{2,1,0:T(8,128)(2,1)}, u32[]{:S(2)}, u32[]{:S(2)}) %all-to-all-start.2) | async-done | bytes 524320 | tf_op jit(solution)/shard_map/while/body/eval_jaxpr/all_to_all | solution.py:143
  413.1 13.4 %all-to-all-done.3 = bf16[8,16,2048]{2,1,0:T(8,128)(2,1)} async-done(((bf16[8,16,2048]{2,1,0:T(8,128)(2,1)}), bf16[8,16,2048]{2,1,0:T(8,128)(2,1)}, u32[]{:S(2)}, u32[]{:S(2)}) %all-to-all-start.3) | async-done | bytes 524320 | tf_op jit(solution)/shard_map/while/body/eval_jaxpr/all_to_all | solution.py:154
  439.5 14.6 %all-to-all-done.2 = bf16[8,16,2048]{2,1,0:T(8,128)(2,1)} async-done(((bf16[8,16,2048]{2,1,0:T(8,128)(2,1)}), bf16[8,16,2048]{2,1,0:T(8,128)(2,1)}, u32[]{:S(2)}, u32[]{:S(2)}) %all-to-all-start.2) | async-done | bytes 524320 | tf_op jit(solution)/shard_map/while/body/eval_jaxpr/all_to_all | solution.py:143
  460.7 14.5 %all-to-all-done.3 = bf16[8,16,2048]{2,1,0:T(8,128)(2,1)} async-done(((bf16[8,16,2048]{2,1,0:T(8,128)(2,1)}), bf16[8,16,2048]{2,1,0:T(8,128)(2,1)}, u32[]{:S(2)}, u32[]{:S(2)}) %all-to-all-start.3) | async-done | bytes 524320 | tf_op jit(solution)/shard_map/while/body/eval_jaxpr/all_to_all | solution.py:154
  488.2 10.3 %all-to-all-done.2 = bf16[8,16,2048]{2,1,0:T(8,128)(2,1)} async-done(((bf16[8,16,2048]{2,1,0:T(8,128)(2,1)}), bf16[8,16,2048]{2,1,0:T(8,128)(2,1)}, u32[]{:S(2)}, u32[]{:S(2)}) %all-to-all-start.2) | async-done | bytes 524320 | tf_op jit(solution)/shard_map/while/body/eval_jaxpr/all_to_all | solution.py:143
  518.3 13.9 %collective-permute-done.1 = bf16[32,2048]{1,0:T(8,128)(2,1)S(1)} collective-permute-done((bf16[32,2048]{1,0:T(8,128)(2,1)S(1)}, bf16[32,2048]{1,0:T(8,128)(2,1)S(1)}, u32[]{:S(2)}, u32[]{:S(2)}) %collective-permute-start.1) | collective-permute-done | bytes 131104 | tf_op jit(solution)/shard_map/while/body/eval_jaxpr/ppermute | solution.py:12
  538.8 10.3 %all-to-all-done.2 = bf16[8,16,2048]{2,1,0:T(8,128)(2,1)} async-done(((bf16[8,16,2048]{2,1,0:T(8,128)(2,1)}), bf16[8,16,2048]{2,1,0:T(8,128)(2,1)}, u32[]{:S(2)}, u32[]{:S(2)}) %all-to-all-start.2) | async-done | bytes 524320 | tf_op jit(solution)/shard_map/while/body/eval_jaxpr/all_to_all | solution.py:143
  575.7 10.6 %collective-permute-done.1 = bf16[32,2048]{1,0:T(8,128)(2,1)S(1)} collective-permute-done((bf16[32,2048]{1,0:T(8,128)(2,1)S(1)}, bf16[32,2048]{1,0:T(8,128)(2,1)S(1)}, u32[]{:S(2)}, u32[]{:S(2)}) %collective-permute-start.1) | collective-permute-done | bytes 131104 | tf_op jit(solution)/shard_map/while/body/eval_jaxpr/ppermute | solution.py:12
  592.9 10.3 %all-to-all-done.2 = bf16[8,16,2048]{2,1,0:T(8,128)(2,1)} async-done(((bf16[8,16,2048]{2,1,0:T(8,128)(2,1)}), bf16[8,16,2048]{2,1,0:T(8,128)(2,1)}, u32[]{:S(2)}, u32[]{:S(2)}) %all-to-all-start.2) | async-done | bytes 524320 | tf_op jit(solution)/shard_map/while/body/eval_jaxpr/all_to_all | solution.py:143
  629.8 10.2 %collective-permute-done.1 = bf16[32,2048]{1,0:T(8,128)(2,1)S(1)} collective-permute-done((bf16[32,2048]{1,0:T(8,128)(2,1)S(1)}, bf16[32,2048]{1,0:T(8,128)(2,1)S(1)}, u32[]{:S(2)}, u32[]{:S(2)}) %collective-permute-start.1) | collective-permute-done | bytes 131104 | tf_op jit(solution)/shard_map/while/body/eval_jaxpr/ppermute | solution.py:12
  646.6 10.3 %all-to-all-done.2 = bf16[8,16,2048]{2,1,0:T(8,128)(2,1)} async-done(((bf16[8,16,2048]{2,1,0:T(8,128)(2,1)}), bf16[8,16,2048]{2,1,0:T(8,128)(2,1)}, u32[]{:S(2)}, u32[]{:S(2)}) %all-to-all-start.2) | async-done | bytes 524320 | tf_op jit(solution)/shard_map/while/body/eval_jaxpr/all_to_all | solution.py:143
  696.9 11.6 %all-to-all-done.2 = bf16[8,16,2048]{2,1,0:T(8,128)(2,1)} async-done(((bf16[8,16,2048]{2,1,0:T(8,128)(2,1)}), bf16[8,16,2048]{2,1,0:T(8,128)(2,1)}, u32[]{:S(2)}, u32[]{:S(2)}) %all-to-all-start.2) | async-done | bytes 524320 | tf_op jit(solution)/shard_map/while/body/eval_jaxpr/all_to_all | solution.py:143
  (289 shorter events, 529.7 us)
Async XLA Ops:
  14.1 21.9 %all-to-all-start = ((bf16[8,16,2048]{2,1,0:T(8,128)(2,1)}), bf16[8,16,2048]{2,1,0:T(8,128)(2,1)}, u32[]{:S(2)}, u32[]{:S(2)}) async-start(bf16[8,16,2048]{2,1,0:T(8,128)(2,1)} %bitcast.174), calls=%async_computation | async-start | bytes 1048576 | tf_op jit(solution)/shard_map/while/body/eval_jaxpr/all_to_all | solution.py:103
  44.4 14.4 %all-to-all-start.1 = ((bf16[8,16,2048]{2,1,0:T(8,128)(2,1)}), bf16[8,16,2048]{2,1,0:T(8,128)(2,1)}, u32[]{:S(2)}, u32[]{:S(2)}) async-start(bf16[8,16,2048]{2,1,0:T(8,128)(2,1)} %bitcast.175), calls=%async_computation.1 | async-start | bytes 1048576 | tf_op jit(solution)/shard_map/while/body/eval_jaxpr/all_to_all | solution.py:124
  69.2 19.0 %all-to-all-start = ((bf16[8,16,2048]{2,1,0:T(8,128)(2,1)}), bf16[8,16,2048]{2,1,0:T(8,128)(2,1)}, u32[]{:S(2)}, u32[]{:S(2)}) async-start(bf16[8,16,2048]{2,1,0:T(8,128)(2,1)} %bitcast.174), calls=%async_computation | async-start | bytes 1048576 | tf_op jit(solution)/shard_map/while/body/eval_jaxpr/all_to_all | solution.py:103
  96.7 18.4 %all-to-all-start.1 = ((bf16[8,16,2048]{2,1,0:T(8,128)(2,1)}), bf16[8,16,2048]{2,1,0:T(8,128)(2,1)}, u32[]{:S(2)}, u32[]{:S(2)}) async-start(bf16[8,16,2048]{2,1,0:T(8,128)(2,1)} %bitcast.175), calls=%async_computation.1 | async-start | bytes 1048576 | tf_op jit(solution)/shard_map/while/body/eval_jaxpr/all_to_all | solution.py:124
  125.4 18.8 %all-to-all-start = ((bf16[8,16,2048]{2,1,0:T(8,128)(2,1)}), bf16[8,16,2048]{2,1,0:T(8,128)(2,1)}, u32[]{:S(2)}, u32[]{:S(2)}) async-start(bf16[8,16,2048]{2,1,0:T(8,128)(2,1)} %bitcast.174), calls=%async_computation | async-start | bytes 1048576 | tf_op jit(solution)/shard_map/while/body/eval_jaxpr/all_to_all | solution.py:103
  152.7 18.5 %all-to-all-start.1 = ((bf16[8,16,2048]{2,1,0:T(8,128)(2,1)}), bf16[8,16,2048]{2,1,0:T(8,128)(2,1)}, u32[]{:S(2)}, u32[]{:S(2)}) async-start(bf16[8,16,2048]{2,1,0:T(8,128)(2,1)} %bitcast.175), calls=%async_computation.1 | async-start | bytes 1048576 | tf_op jit(solution)/shard_map/while/body/eval_jaxpr/all_to_all | solution.py:124
  181.4 18.9 %all-to-all-start = ((bf16[8,16,2048]{2,1,0:T(8,128)(2,1)}), bf16[8,16,2048]{2,1,0:T(8,128)(2,1)}, u32[]{:S(2)}, u32[]{:S(2)}) async-start(bf16[8,16,2048]{2,1,0:T(8,128)(2,1)} %bitcast.174), calls=%async_computation | async-start | bytes 1048576 | tf_op jit(solution)/shard_map/while/body/eval_jaxpr/all_to_all | solution.py:103
  208.8 18.5 %all-to-all-start.1 = ((bf16[8,16,2048]{2,1,0:T(8,128)(2,1)}), bf16[8,16,2048]{2,1,0:T(8,128)(2,1)}, u32[]{:S(2)}, u32[]{:S(2)}) async-start(bf16[8,16,2048]{2,1,0:T(8,128)(2,1)} %bitcast.175), calls=%async_computation.1 | async-start | bytes 1048576 | tf_op jit(solution)/shard_map/while/body/eval_jaxpr/all_to_all | solution.py:124
  237.5 18.9 %all-to-all-start = ((bf16[8,16,2048]{2,1,0:T(8,128)(2,1)}), bf16[8,16,2048]{2,1,0:T(8,128)(2,1)}, u32[]{:S(2)}, u32[]{:S(2)}) async-start(bf16[8,16,2048]{2,1,0:T(8,128)(2,1)} %bitcast.174), calls=%async_computation | async-start | bytes 1048576 | tf_op jit(solution)/shard_map/while/body/eval_jaxpr/all_to_all | solution.py:103
  258.8 14.8 %all-to-all-start.1 = ((bf16[8,16,2048]{2,1,0:T(8,128)(2,1)}), bf16[8,16,2048]{2,1,0:T(8,128)(2,1)}, u32[]{:S(2)}, u32[]{:S(2)}) async-start(bf16[8,16,2048]{2,1,0:T(8,128)(2,1)} %bitcast.175), calls=%async_computation.1 | async-start | bytes 1048576 | tf_op jit(solution)/shard_map/while/body/eval_jaxpr/all_to_all | solution.py:124
  289.3 19.3 %all-to-all-start = ((bf16[8,16,2048]{2,1,0:T(8,128)(2,1)}), bf16[8,16,2048]{2,1,0:T(8,128)(2,1)}, u32[]{:S(2)}, u32[]{:S(2)}) async-start(bf16[8,16,2048]{2,1,0:T(8,128)(2,1)} %bitcast.174), calls=%async_computation | async-start | bytes 1048576 | tf_op jit(solution)/shard_map/while/body/eval_jaxpr/all_to_all | solution.py:103
  311.1 18.5 %all-to-all-start.1 = ((bf16[8,16,2048]{2,1,0:T(8,128)(2,1)}), bf16[8,16,2048]{2,1,0:T(8,128)(2,1)}, u32[]{:S(2)}, u32[]{:S(2)}) async-start(bf16[8,16,2048]{2,1,0:T(8,128)(2,1)} %bitcast.175), calls=%async_computation.1 | async-start | bytes 1048576 | tf_op jit(solution)/shard_map/while/body/eval_jaxpr/all_to_all | solution.py:124
  339.6 19.1 %all-to-all-start = ((bf16[8,16,2048]{2,1,0:T(8,128)(2,1)}), bf16[8,16,2048]{2,1,0:T(8,128)(2,1)}, u32[]{:S(2)}, u32[]{:S(2)}) async-start(bf16[8,16,2048]{2,1,0:T(8,128)(2,1)} %bitcast.174), calls=%async_computation | async-start | bytes 1048576 | tf_op jit(solution)/shard_map/while/body/eval_jaxpr/all_to_all | solution.py:103
  361.1 18.4 %all-to-all-start.1 = ((bf16[8,16,2048]{2,1,0:T(8,128)(2,1)}), bf16[8,16,2048]{2,1,0:T(8,128)(2,1)}, u32[]{:S(2)}, u32[]{:S(2)}) async-start(bf16[8,16,2048]{2,1,0:T(8,128)(2,1)} %bitcast.175), calls=%async_computation.1 | async-start | bytes 1048576 | tf_op jit(solution)/shard_map/while/body/eval_jaxpr/all_to_all | solution.py:124
  388.2 18.9 %all-to-all-start.2 = ((bf16[8,16,2048]{2,1,0:T(8,128)(2,1)}), bf16[8,16,2048]{2,1,0:T(8,128)(2,1)}, u32[]{:S(2)}, u32[]{:S(2)}) async-start(bf16[8,16,2048]{2,1,0:T(8,128)(2,1)} %bitcast.173), calls=%async_computation.2 | async-start | bytes 1048576 | tf_op jit(solution)/shard_map/while/body/eval_jaxpr/all_to_all | solution.py:143
  408.0 18.4 %all-to-all-start.3 = ((bf16[8,16,2048]{2,1,0:T(8,128)(2,1)}), bf16[8,16,2048]{2,1,0:T(8,128)(2,1)}, u32[]{:S(2)}, u32[]{:S(2)}) async-start(bf16[8,16,2048]{2,1,0:T(8,128)(2,1)} %bitcast.176), calls=%async_computation.3 | async-start | bytes 1048576 | tf_op jit(solution)/shard_map/while/body/eval_jaxpr/all_to_all | solution.py:154
  435.3 18.8 %all-to-all-start.2 = ((bf16[8,16,2048]{2,1,0:T(8,128)(2,1)}), bf16[8,16,2048]{2,1,0:T(8,128)(2,1)}, u32[]{:S(2)}, u32[]{:S(2)}) async-start(bf16[8,16,2048]{2,1,0:T(8,128)(2,1)} %bitcast.173), calls=%async_computation.2 | async-start | bytes 1048576 | tf_op jit(solution)/shard_map/while/body/eval_jaxpr/all_to_all | solution.py:143
  455.0 20.2 %all-to-all-start.3 = ((bf16[8,16,2048]{2,1,0:T(8,128)(2,1)}), bf16[8,16,2048]{2,1,0:T(8,128)(2,1)}, u32[]{:S(2)}, u32[]{:S(2)}) async-start(bf16[8,16,2048]{2,1,0:T(8,128)(2,1)} %bitcast.176), calls=%async_computation.3 | async-start | bytes 1048576 | tf_op jit(solution)/shard_map/while/body/eval_jaxpr/all_to_all | solution.py:154
  484.0 14.4 %all-to-all-start.2 = ((bf16[8,16,2048]{2,1,0:T(8,128)(2,1)}), bf16[8,16,2048]{2,1,0:T(8,128)(2,1)}, u32[]{:S(2)}, u32[]{:S(2)}) async-start(bf16[8,16,2048]{2,1,0:T(8,128)(2,1)} %bitcast.173), calls=%async_computation.2 | async-start | bytes 1048576 | tf_op jit(solution)/shard_map/while/body/eval_jaxpr/all_to_all | solution.py:143
  517.0 15.2 %collective-permute-start.1 = (bf16[32,2048]{1,0:T(8,128)(2,1)S(1)}, bf16[32,2048]{1,0:T(8,128)(2,1)S(1)}, u32[]{:S(2)}, u32[]{:S(2)}) collective-permute-start(bf16[32,2048]{1,0:T(8,128)(2,1)S(1)} %get-tuple-element.1025), channel_id=1, source_target_pairs={{8,0},{16,8},{24,16},{9,1},{17,9},{25,17},{10,2},{18,10},{26,18},{... | collective-permute-start | bytes 393224 | tf_op jit(solution)/shard_map/while/body/eval_jaxpr/ppermute | solution.py:12
  642.4 14.5 %all-to-all-start.2 = ((bf16[8,16,2048]{2,1,0:T(8,128)(2,1)}), bf16[8,16,2048]{2,1,0:T(8,128)(2,1)}, u32[]{:S(2)}, u32[]{:S(2)}) async-start(bf16[8,16,2048]{2,1,0:T(8,128)(2,1)} %bitcast.173), calls=%async_computation.2 | async-start | bytes 1048576 | tf_op jit(solution)/shard_map/while/body/eval_jaxpr/all_to_all | solution.py:143
  664.5 14.8 %all-to-all-start.3 = ((bf16[8,16,2048]{2,1,0:T(8,128)(2,1)}), bf16[8,16,2048]{2,1,0:T(8,128)(2,1)}, u32[]{:S(2)}, u32[]{:S(2)}) async-start(bf16[8,16,2048]{2,1,0:T(8,128)(2,1)} %bitcast.176), calls=%async_computation.3 | async-start | bytes 1048576 | tf_op jit(solution)/shard_map/while/body/eval_jaxpr/all_to_all | solution.py:154
  692.8 15.8 %all-to-all-start.2 = ((bf16[8,16,2048]{2,1,0:T(8,128)(2,1)}), bf16[8,16,2048]{2,1,0:T(8,128)(2,1)}, u32[]{:S(2)}, u32[]{:S(2)}) async-start(bf16[8,16,2048]{2,1,0:T(8,128)(2,1)} %bitcast.173), calls=%async_computation.2 | async-start | bytes 1048576 | tf_op jit(solution)/shard_map/while/body/eval_jaxpr/all_to_all | solution.py:143
  716.2 17.5 %all-to-all-start.3 = ((bf16[8,16,2048]{2,1,0:T(8,128)(2,1)}), bf16[8,16,2048]{2,1,0:T(8,128)(2,1)}, u32[]{:S(2)}, u32[]{:S(2)}) async-start(bf16[8,16,2048]{2,1,0:T(8,128)(2,1)} %bitcast.176), calls=%async_computation.3 | async-start | bytes 1048576 | tf_op jit(solution)/shard_map/while/body/eval_jaxpr/all_to_all | solution.py:154
  (38 other events, 184.6 us)
where the time goes:
time: 746 us; the launch traced here: 740 us
  waiting for transfers between devices  369 us (49%)
  starting transfers between devices  147 us (20%)
  matrix products  115 us (15%)
  local copies, waits for them, and re-layouts  64.1 us (9%)
  other arithmetic  43.5 us (6%)
    all_to_all x7, waiting for transfers between devices, forward_layer(): lax.all_to_all(sending.reshape(experts, capacity, width), 'expert', split...  104 us
    all_to_all x7, waiting for transfers between devices, backward_layer(): lax.all_to_all(grad_rows, 'expert', split_axis=0, concat_axis=0, tiled=True)  82.1 us
    all_to_all x7, waiting for transfers between devices, backward_layer(): lax.all_to_all(d_rows.reshape(experts, capacity, width), 'expert', split_...  75 us
    all_to_all x7, waiting for transfers between devices, forward_layer(): lax.all_to_all(out.reshape(sources, count, dim), 'expert', split_axis=0,...  61.1 us
    ppermute x14, waiting for transfers between devices, passed_along(): return lax.ppermute(shard, axis, pairs)  47.2 us
    dynamic_slice x35, local copies, waits for them, and re-layouts, keep_row(): old = lax.dynamic_index_in_dim(store, index, 0, keepdims=False)  44.1 us
    dynamic_update_slice x21, other arithmetic, keep_row(): return lax.dynamic_update_index_in_dim(store, fresh, index, 0)  39.7 us
    all_to_all x7, starting transfers between devices, backward_layer(): lax.all_to_all(d_rows.reshape(experts, capacity, width), 'expert', split_...  32.7 us
  transfers between devices with their start and end apart: 42, of which 35 were waited for; matrix products, arithmetic and copies ran while one was open for 7% of the time, Pallas kernels for 0%

commit v1 on v0

--- a/solution.py
+++ b/solution.py
@@ -1,6 +1,10 @@
+import functools
+
 import jax
 import jax.numpy as jnp
 from jax import lax
+from jax.experimental import pallas as pl
+from jax.experimental.pallas import tpu as pltpu
 from jax.sharding import PartitionSpec as P
 
 EPS = 1e-06
@@ -80,7 +84,7 @@
     return (dispatch, combine)
 
 
-def shards(inputs, cotangent, norm_gain, w_gate, w_up, w_down, route_ids, route_weights):
+def shards_padded(inputs, cotangent, norm_gain, w_gate, w_up, w_down, route_ids, route_weights):
     sections = lax.axis_size("section")
     section = lax.axis_index("section")
     experts = lax.axis_size("expert")
@@ -214,6 +218,329 @@
     layer_outputs = forward_state[2][None]
     input_grads = backward_state[1][None]
     return (layer_outputs, input_grads)
+
+
+def route_masks(ids, weights, capacity, slots):
+    rows = ids.shape[0]
+    column = lax.broadcasted_iota(jnp.int32, (rows, slots), 1)
+    expert = column // capacity
+    place = (column - expert * capacity).astype(jnp.float32)
+    first = ids[:, 0:1] == expert
+    second = ids[:, 1:2] == expert
+    named = jnp.where(first | second, 1.0, 0.0)
+    below = lax.broadcasted_iota(jnp.int32, (rows, rows), 0) > lax.broadcasted_iota(
+        jnp.int32, (rows, rows), 1
+    )
+    earlier = jnp.dot(
+        jnp.where(below, 1.0, 0.0).astype(jnp.bfloat16),
+        named.astype(jnp.bfloat16),
+        preferred_element_type=jnp.float32,
+    )
+    pick = jnp.where(earlier == place, named, 0.0)
+    mix = pick * jnp.where(first, weights[:, 0:1], weights[:, 1:2])
+    high = mix.astype(jnp.bfloat16)
+    low = (mix - high.astype(jnp.float32)).astype(jnp.bfloat16)
+    return (pick.astype(jnp.bfloat16), high, low)
+
+
+def kernel(
+    sections,
+    experts,
+    capacity,
+    x_ref,
+    ct_ref,
+    gain_ref,
+    ids_ref,
+    wts_ref,
+    wg_hbm,
+    wu_hbm,
+    wd_hbm,
+    out_ref,
+    grad_ref,
+    wg,
+    wu,
+    wd,
+    act,
+    upg,
+    send,
+    recv,
+    gates,
+    ups,
+    pick_s,
+    high_s,
+    low_s,
+    hid_a,
+    hid_b,
+    w_sem,
+    send_sem,
+    recv_sem,
+    pass_send,
+    pass_recv,
+):
+    section = lax.axis_index("section")
+    me = lax.axis_index("expert")
+    last = sections - 1
+    micro, rows, width = x_ref.shape
+    slots = experts * capacity
+    hid = wg.shape[1]
+    tile = 256
+    bf16, f32 = jnp.bfloat16, jnp.float32
+
+    loads = [
+        pltpu.make_async_copy(src, dst, w_sem.at[i])
+        for i, (src, dst) in enumerate(((wg_hbm, wg), (wu_hbm, wu), (wd_hbm, wd)))
+    ]
+    for load in loads:
+        load.start()
+
+    barrier = pltpu.get_barrier_semaphore()
+    for off in range(1, experts):
+        pl.semaphore_signal(
+            barrier,
+            inc=1,
+            device_id=(section, lax.rem(me + off, experts)),
+            device_id_type=pl.DeviceIdType.MESH,
+        )
+
+    @pl.when(section > 0)
+    def _():
+        pl.semaphore_signal(
+            barrier, inc=1, device_id=(section - 1, me), device_id_type=pl.DeviceIdType.MESH
+        )
+
+    @pl.when(section < last)
+    def _():
+        pl.semaphore_signal(
+            barrier, inc=1, device_id=(section + 1, me), device_id_type=pl.DeviceIdType.MESH
+        )
+
+    gain = gain_ref[...].astype(f32)
+
+    @pl.when(section == 0)
+    def _():
+        act[...] = x_ref[...]
+
+    @pl.when(section == last)
+    def _():
+        upg[...] = ct_ref[...]
+
+    for m in range(micro):
+        pick, high, low = route_masks(ids_ref[m], wts_ref[m], capacity, slots)
+        pick_s[m] = pick
+        high_s[m] = high
+        low_s[m] = low
+
+    neighbours = jnp.where(section > 0, 1, 0) + jnp.where(section < last, 1, 0)
+    pl.semaphore_wait(barrier, experts - 1 + neighbours)
+
+    def block(index):
+        return pl.ds(pl.multiple_of(index * capacity, capacity), capacity)
+
+    def exchange(kind, m):
+        for off in range(1, experts):
+            peer = lax.rem(me + off, experts)
+            pltpu.make_async_remote_copy(
+                src_ref=send.at[kind, m, block(peer)],
+                dst_ref=recv.at[kind, m, block(me)],
+                send_sem=send_sem.at[kind, m],
+                recv_sem=recv_sem.at[kind, m],
+                device_id=(section, peer),
+                device_id_type=pl.DeviceIdType.MESH,
+            ).start()
+        own = pltpu.make_async_copy(
+            send.at[kind, m, block(me)], recv.at[kind, m, block(me)], recv_sem.at[kind, m]
+        )
+        own.start()
+
+    def arrive(kind, m):
+        pltpu.make_async_copy(
+            recv.at[kind, m], recv.at[kind, m], recv_sem.at[kind, m]
+        ).wait()
+
+    def sent(kind, m):
+        part = send.at[kind, m, pl.ds(0, (experts - 1) * capacity)]
+        pltpu.make_async_copy(part, part, send_sem.at[kind, m]).wait()
+
+    def pass_on(src, dst, which, m, to):
+        return pltpu.make_async_remote_copy(
+            src_ref=src.at[m],
+            dst_ref=dst.at[m],
+            send_sem=pass_send.at[which, m],
+            recv_sem=pass_recv.at[which, m],
+            device_id=(to, me),
+            device_id_type=pl.DeviceIdType.MESH,
+        )
+
+    def first_dims(left, right):
+        return lax.dot_general(
+            left, right, (((0,), (0,)), ((), ())), preferred_element_type=f32
+        )
+
+    def normed_parts(m):
+        values = act[m].astype(f32)
+        scale = lax.rsqrt(jnp.mean(values * values, axis=-1, keepdims=True) + EPS)
+        return values, scale
+
+    def forward(m, carry):
+        @pl.when(section > 0)
+        def _():
+            pass_on(out_ref, act, 0, m, section).wait_recv()
+
+        values, scale = normed_parts(m)
+        normed = (values * scale * gain).astype(bf16)
+        send[0, m] = first_dims(pick_s[m], normed).astype(bf16)
+        exchange(0, m)
+
+        @pl.when(m == 0)
+        def _():
+            for load in loads:
+                load.wait()
+
+        arrive(0, m)
+        for at in range(0, hid, tile):
+            cols = pl.ds(at, tile)
+            gate = jnp.dot(recv[0, m], wg[:, cols], preferred_element_type=f32)
+            up = jnp.dot(recv[0, m], wu[:, cols], preferred_element_type=f32)
+            gates[m, :, cols] = gate
+            ups[m, :, cols] = up
+            hid_a[:, cols] = (gate * jax.nn.sigmoid(gate) * up).astype(bf16)
+        for at in range(0, width, tile):
+            cols = pl.ds(at, tile)
+            send[1, m, :, cols] = jnp.dot(
+                hid_a[...], wd[:, cols], preferred_element_type=f32
+            ).astype(bf16)
+        exchange(1, m)
+        arrive(1, m)
+        back = recv[1, m]
+        branch = jnp.dot(high_s[m], back, preferred_element_type=f32) + jnp.dot(
+            low_s[m], back, preferred_element_type=f32
+        )
+        out_ref[m] = (act[m].astype(f32) + branch).astype(bf16)
+
+        @pl.when(section < last)
+        def _():
+            pass_on(out_ref, act, 0, m, section + 1).start()
+
+        return carry
+
+    lax.fori_loop(0, micro, forward, 0)
+
+    def backward(m, carry):
+        @pl.when(section < last)
+        def _():
+            pass_on(grad_ref, upg, 1, m, section).wait_recv()
+
+        dy = upg[m]
+        send[2, m] = (first_dims(high_s[m], dy) + first_dims(low_s[m], dy)).astype(bf16)
+        exchange(2, m)
+        arrive(2, m)
+        for at in range(0, hid, tile):
+            cols = pl.ds(at, tile)
+            d_hidden = contract_last(recv[2, m], wd[cols, :])
+            gate = gates[m, :, cols]
+            up = ups[m, :, cols]
+            sig = jax.nn.sigmoid(gate)
+            hid_a[:, cols] = (d_hidden * up * sig * (1.0 + gate * (1.0 - sig))).astype(bf16)
+            hid_b[:, cols] = (d_hidden * gate * sig).astype(bf16)
+        for at in range(0, width, tile):
+            cols = pl.ds(at, tile)
+            send[3, m, :, cols] = (
+                contract_last(hid_a[...], wg[cols, :]) + contract_last(hid_b[...], wu[cols, :])
+            ).astype(bf16)
+        exchange(3, m)
+        arrive(3, m)
+        d_normed = jnp.dot(pick_s[m], recv[3, m], preferred_element_type=f32)
+        values, scale = normed_parts(m)
+        scaled = d_normed * gain
+        inner = jnp.mean(scaled * values, axis=-1, keepdims=True)
+        grad_ref[m] = (
+            upg[m].astype(f32) + scale * scaled - values * scale * scale * scale * inner
+        ).astype(bf16)
+
+        @pl.when(section > 0)
+        def _():
+            pass_on(grad_ref, upg, 1, m, section - 1).start()
+
+        return carry
+
+    lax.fori_loop(0, micro, backward, 0)
+
+    def finish(m, carry):
+        for kind in range(4):
+            sent(kind, m)
+
+        @pl.when(section < last)
+        def _():
+            pass_on(out_ref, act, 0, m, section + 1).wait_send()
+
+        @pl.when(section > 0)
+        def _():
+            pass_on(grad_ref, upg, 1, m, section - 1).wait_send()
+
+        return carry
+
+    lax.fori_loop(0, micro, finish, 0)
+
+
+def shards(inputs, cotangent, norm_gain, w_gate, w_up, w_down, route_ids, route_weights):
+    sections = lax.axis_size("section")
+    experts = lax.axis_size("expert")
+    micro, rows, width = inputs.shape
+    top = route_ids.shape[3]
+    hid = w_gate.shape[3]
+    capacity = 2 * rows * top // experts
+    slots = experts * capacity
+    if capacity % 16:
+        return shards_padded(
+            inputs, cotangent, norm_gain, w_gate, w_up, w_down, route_ids, route_weights
+        )
+    bf16, f32 = jnp.bfloat16, jnp.float32
+    vmem = pl.BlockSpec(memory_space=pltpu.VMEM)
+    anywhere = pl.BlockSpec(memory_space=pl.ANY)
+    kinds = 4
+    outs = pl.pallas_call(
+        functools.partial(kernel, sections, experts, capacity),
+        out_shape=(
+            jax.ShapeDtypeStruct((micro, rows, width), bf16),
+            jax.ShapeDtypeStruct((micro, rows, width), bf16),
+        ),
+        in_specs=[vmem] * 5 + [anywhere] * 3,
+        out_specs=(vmem, vmem),
+        scratch_shapes=[
+            pltpu.VMEM((width, hid), bf16),
+            pltpu.VMEM((width, hid), bf16),
+            pltpu.VMEM((hid, width), bf16),
+            pltpu.VMEM((micro, rows, width), bf16),
+            pltpu.VMEM((micro, rows, width), bf16),
+            pltpu.VMEM((kinds, micro, slots, width), bf16),
+            pltpu.VMEM((kinds, micro, slots, width), bf16),
+            pltpu.VMEM((micro, slots, hid), f32),
+            pltpu.VMEM((micro, slots, hid), f32),
+            pltpu.VMEM((micro, rows, slots), bf16),
+            pltpu.VMEM((micro, rows, slots), bf16),
+            pltpu.VMEM((micro, rows, slots), bf16),
+            pltpu.VMEM((slots, hid), bf16),
+            pltpu.VMEM((slots, hid), bf16),
+            pltpu.SemaphoreType.DMA((3,)),
+            pltpu.SemaphoreType.DMA((kinds, micro)),
+            pltpu.SemaphoreType.DMA((kinds, micro)),
+            pltpu.SemaphoreType.DMA((2, micro)),
+            pltpu.SemaphoreType.DMA((2, micro)),
+        ],
+        compiler_params=pltpu.CompilerParams(
+            collective_id=0, has_side_effects=True, vmem_limit_bytes=56 * 2**20
+        ),
+    )(
+        inputs,
+        cotangent,
+        norm_gain,
+        route_ids[0],
+        route_weights[0],
+        w_gate[0, 0],
+        w_up[0, 0],
+        w_down[0, 0],
+    )
+    return (outs[0][None], outs[1][None])
 
 
 def solution(mesh):

time: 746 us -> 363 us (0.49)
  waiting for transfers between devices: 369 us -> 0 us
  Pallas kernels: 0 us -> 355 us
  starting transfers between devices: 147 us -> 0 us
  matrix products: 115 us -> 0 us
  local copies, waits for them, and re-layouts: 64.1 us -> 6.59 us
  other arithmetic: 43.5 us -> 0 us
    pallas_call x0 -> x1, Pallas kernels: none -> 355 us  [shards(): pl.pallas_call(functools.partial(kernel, sections, experts, capacity), ou...]
    all_to_all x28 -> x0, waiting for transfers between devices: 322 us -> none  [the longest x7 104 us: forward_layer(): lax.all_to_all(sending.reshape(experts, capacity, width), 'expert', split...]
    all_to_all x28 -> x0, starting transfers between devices: 123 us -> none  [the longest x7 32.7 us: backward_layer(): lax.all_to_all(d_rows.reshape(experts, capacity, width), 'expert', split_...]
    dot_general x52 -> x0, matrix products: 115 us -> none  [the longest x12 30.4 us: contract_last(): lax.dot_general(left, right, (((1,), (1,)), ((), ())), preferred_element_...]
    ppermute x14 -> x0, waiting for transfers between devices: 47.2 us -> none  [passed_along(): return lax.ppermute(shard, axis, pairs)]
    dynamic_slice x35 -> x0, local copies, waits for them, and re-layouts: 44.1 us -> none  [keep_row(): old = lax.dynamic_index_in_dim(store, index, 0, keepdims=False)]
    dynamic_update_slice x21 -> x0, other arithmetic: 39.7 us -> none  [keep_row(): return lax.dynamic_update_index_in_dim(store, fresh, index, 0)]
    ppermute x14 -> x0, starting transfers between devices: 23.7 us -> none  [passed_along(): return lax.ppermute(shard, axis, pairs)]
  transfers between devices with their start and end apart: 42 -> 0, of which waited for: 35 -> 0; matrix products, arithmetic and copies ran while one was open for 7% -> 0% of each run, Pallas kernels for 0% -> 0%
where the time goes in v1:
time: 363 us; the launch traced here: 362 us
  Pallas kernels  355 us (98%)
  local copies, waits for them, and re-layouts  6.59 us (2%)
    pallas_call x1, Pallas kernels, shards(): pl.pallas_call(functools.partial(kernel, sections, experts, capacity), ou...  355 us

profile of v1, /device:TPU:0, one launch (start us, length us, event | category | flops | bytes accessed | tf_op | source)
XLA Modules:
  0.0 362.4 jit_solution(9832788813018161935)
XLA Ops:
  0.6 1.4 copy.10
  2.0 1.4 copy.11
  3.5 355.1 %shard_map.95 = (bf16[4,32,2048]{2,1,0:T(8,128)(2,1)}, bf16[4,32,2048]{2,1,0:T(8,128)(2,1)}) custom-call(bf16[4,32,2048]{2,1,0:T(8,128)(2,1)} %x_ref.1, bf16[4,32,2048]{2,1,0:T(8,128)(2,1)} %ct_ref.1, bf16[1,2048]{1,0:T(2,128)(2,1)} %gain_ref.1, s32[4,32,2]{2,1,0:T(8,128)} %bitcast.12, f32[4,32,2]{2,1,0:T(8,128)} %bitcast.13, bf16[2048,768]{1,0:T(8,128)(2,1)} %bitcast.7, ...), custom_call_target="tpu_custom_call" | custom-call | tf_op jit(solution)/shard_map/pallas_call | solution.py:501
  358.6 1.9 copy.14
  360.5 1.9 copy.15

commit v2 on v1

--- a/solution.py
+++ b/solution.py
@@ -8,6 +8,7 @@
 from jax.sharding import PartitionSpec as P
 
 EPS = 1e-06
+PARTS = 2
 
 
 def passed_along(shard, axis, by):
@@ -271,6 +272,7 @@
     low_s,
     hid_a,
     hid_b,
+    hid_f,
     w_sem,
     send_sem,
     recv_sem,
@@ -284,6 +286,8 @@
     slots = experts * capacity
     hid = wg.shape[1]
     tile = 256
+    parts = PARTS
+    chunk = width // parts
     bf16, f32 = jnp.bfloat16, jnp.float32
 
     loads = [
@@ -336,37 +340,41 @@
     def block(index):
         return pl.ds(pl.multiple_of(index * capacity, capacity), capacity)
 
-    def exchange(kind, m):
+    def span(part):
+        return pl.ds(part * chunk, chunk)
+
+    def exchange(kind, m, part):
+        cols = span(part)
         for off in range(1, experts):
             peer = lax.rem(me + off, experts)
             pltpu.make_async_remote_copy(
-                src_ref=send.at[kind, m, block(peer)],
-                dst_ref=recv.at[kind, m, block(me)],
-                send_sem=send_sem.at[kind, m],
-                recv_sem=recv_sem.at[kind, m],
+                src_ref=send.at[kind, m, block(peer), cols],
+                dst_ref=recv.at[kind, m, block(me), cols],
+                send_sem=send_sem.at[kind, m, part],
+                recv_sem=recv_sem.at[kind, m, part],
                 device_id=(section, peer),
                 device_id_type=pl.DeviceIdType.MESH,
             ).start()
-        own = pltpu.make_async_copy(
-            send.at[kind, m, block(me)], recv.at[kind, m, block(me)], recv_sem.at[kind, m]
-        )
-        own.start()
-
-    def arrive(kind, m):
         pltpu.make_async_copy(
-            recv.at[kind, m], recv.at[kind, m], recv_sem.at[kind, m]
-        ).wait()
-
-    def sent(kind, m):
-        part = send.at[kind, m, pl.ds(0, (experts - 1) * capacity)]
-        pltpu.make_async_copy(part, part, send_sem.at[kind, m]).wait()
-
-    def pass_on(src, dst, which, m, to):
+            send.at[kind, m, block(me), cols],
+            recv.at[kind, m, block(me), cols],
+            recv_sem.at[kind, m, part],
+        ).start()
+
+    def arrive(kind, m, part):
+        whole = recv.at[kind, m, pl.ds(0, slots), span(part)]
+        pltpu.make_async_copy(whole, whole, recv_sem.at[kind, m, part]).wait()
+
+    def sent(kind, m, part):
+        most = send.at[kind, m, pl.ds(0, (experts - 1) * capacity), span(part)]
+        pltpu.make_async_copy(most, most, send_sem.at[kind, m, part]).wait()
+
+    def pass_on(src, dst, which, m, part, to):
         return pltpu.make_async_remote_copy(
-            src_ref=src.at[m],
-            dst_ref=dst.at[m],
-            send_sem=pass_send.at[which, m],
-            recv_sem=pass_recv.at[which, m],
+            src_ref=src.at[m, pl.ds(0, rows), span(part)],
+            dst_ref=dst.at[m, pl.ds(0, rows), span(part)],
+            send_sem=pass_send.at[which, m, part],
+            recv_sem=pass_recv.at[which, m, part],
             device_id=(to, me),
             device_id_type=pl.DeviceIdType.MESH,
         )
@@ -381,101 +389,158 @@
         scale = lax.rsqrt(jnp.mean(values * values, axis=-1, keepdims=True) + EPS)
         return values, scale
 
-    def forward(m, carry):
+    def forward_send(m):
         @pl.when(section > 0)
         def _():
-            pass_on(out_ref, act, 0, m, section).wait_recv()
+            for part in range(parts):
+                pass_on(out_ref, act, 0, m, part, section).wait_recv()
 
         values, scale = normed_parts(m)
         normed = (values * scale * gain).astype(bf16)
-        send[0, m] = first_dims(pick_s[m], normed).astype(bf16)
-        exchange(0, m)
+        for part in range(parts):
+            piece = normed[:, part * chunk : (part + 1) * chunk]
+            send[0, m, :, span(part)] = first_dims(pick_s[m], piece).astype(bf16)
+            exchange(0, m, part)
 
         @pl.when(m == 0)
         def _():
             for load in loads:
                 load.wait()
 
-        arrive(0, m)
-        for at in range(0, hid, tile):
-            cols = pl.ds(at, tile)
-            gate = jnp.dot(recv[0, m], wg[:, cols], preferred_element_type=f32)
-            up = jnp.dot(recv[0, m], wu[:, cols], preferred_element_type=f32)
-            gates[m, :, cols] = gate
-            ups[m, :, cols] = up
-            hid_a[:, cols] = (gate * jax.nn.sigmoid(gate) * up).astype(bf16)
-        for at in range(0, width, tile):
-            cols = pl.ds(at, tile)
-            send[1, m, :, cols] = jnp.dot(
-                hid_a[...], wd[:, cols], preferred_element_type=f32
+    def forward_expert(m):
+        for part in range(parts):
+            arrive(0, m, part)
+            for at in range(0, hid, tile):
+                cols = pl.ds(at, tile)
+                rows_in = recv[0, m, :, span(part)]
+                gate = jnp.dot(rows_in, wg[span(part), cols], preferred_element_type=f32)
+                up = jnp.dot(rows_in, wu[span(part), cols], preferred_element_type=f32)
+                if part > 0:
+                    gate = gates[m, :, cols] + gate
+                    up = ups[m, :, cols] + up
+                gates[m, :, cols] = gate
+                ups[m, :, cols] = up
+                if part == parts - 1:
+                    hid_a[:, cols] = (gate * jax.nn.sigmoid(gate) * up).astype(bf16)
+        for part in range(parts):
+            for at in range(part * chunk, (part + 1) * chunk, tile):
+                cols = pl.ds(at, tile)
+                send[1, m, :, cols] = jnp.dot(
+                    hid_a[...], wd[:, cols], preferred_element_type=f32
+                ).astype(bf16)
+            exchange(1, m, part)
+
+    def forward_finish(m):
+        for part in range(parts):
+            arrive(1, m, part)
+            back = recv[1, m, :, span(part)]
+            branch = jnp.dot(high_s[m], back, preferred_element_type=f32) + jnp.dot(
+                low_s[m], back, preferred_element_type=f32
+            )
+            out_ref[m, :, span(part)] = (
+                act[m, :, span(part)].astype(f32) + branch
             ).astype(bf16)
-        exchange(1, m)
-        arrive(1, m)
-        back = recv[1, m]
-        branch = jnp.dot(high_s[m], back, preferred_element_type=f32) + jnp.dot(
-            low_s[m], back, preferred_element_type=f32
-        )
-        out_ref[m] = (act[m].astype(f32) + branch).astype(bf16)
-
-        @pl.when(section < last)
-        def _():
-            pass_on(out_ref, act, 0, m, section + 1).start()
-
+
+            @pl.when(section < last)
+            def _():
+                pass_on(out_ref, act, 0, m, part, section + 1).start()
+
+    def backward_send(m):
+        for part in range(parts):
+
+            @pl.when(section < last)
+            def _():
+                pass_on(grad_ref, upg, 1, m, part, section).wait_recv()
+
+            dy = upg[m, :, span(part)]
+            send[2, m, :, span(part)] = (
+                first_dims(high_s[m], dy) + first_dims(low_s[m], dy)
+            ).astype(bf16)
+            exchange(2, m, part)
+
+    def backward_expert(m):
+        for part in range(parts):
+            arrive(2, m, part)
+            for at in range(0, hid, tile):
+                cols = pl.ds(at, tile)
+                d_hidden = contract_last(recv[2, m, :, span(part)], wd[cols, span(part)])
+                if part > 0:
+                    d_hidden = hid_f[:, cols] + d_hidden
+                if part < parts - 1:
+                    hid_f[:, cols] = d_hidden
+                else:
+                    gate = gates[m, :, cols]
+                    up = ups[m, :, cols]
+                    sig = jax.nn.sigmoid(gate)
+                    hid_a[:, cols] = (
+                        d_hidden * up * sig * (1.0 + gate * (1.0 - sig))
+                    ).astype(bf16)
+                    hid_b[:, cols] = (d_hidden * gate * sig).astype(bf16)
+        for part in range(parts):
+            for at in range(part * chunk, (part + 1) * chunk, tile):
+                cols = pl.ds(at, tile)
+                send[3, m, :, cols] = (
+                    contract_last(hid_a[...], wg[cols, :])
+                    + contract_last(hid_b[...], wu[cols, :])
+                ).astype(bf16)
+            exchange(3, m, part)
+
+    def backward_finish(m):
+        values, scale = normed_parts(m)
+        pieces = []
+        total = jnp.zeros((rows, 1), f32)
+        for part in range(parts):
+            arrive(3, m, part)
+            d_normed = jnp.dot(
+                pick_s[m], recv[3, m, :, span(part)], preferred_element_type=f32
+            )
+            at, to = part * chunk, (part + 1) * chunk
+            scaled = d_normed * gain[:, at:to]
+            total = total + jnp.sum(scaled * values[:, at:to], axis=-1, keepdims=True)
+            pieces.append(scaled)
+        inner = scale * scale * scale * (total / width)
+        for part in range(parts):
+            at, to = part * chunk, (part + 1) * chunk
+            grad_ref[m, :, span(part)] = (
+                upg[m, :, span(part)].astype(f32)
+                + scale * pieces[part]
+                - values[:, at:to] * inner
+            ).astype(bf16)
+
+            @pl.when(section > 0)
+            def _():
+                pass_on(grad_ref, upg, 1, m, part, section - 1).start()
+
+    def tick(step, carry):
+        ahead = step - section
+        behind = step - (2 * sections - 1 - section)
+        runs_ahead = jnp.logical_and(ahead >= 0, ahead < micro)
+        runs_behind = jnp.logical_and(behind >= 0, behind < micro)
+        fm = jnp.clip(ahead, 0, micro - 1)
+        bm = jnp.clip(behind, 0, micro - 1)
+        for forward_part, backward_part in (
+            (forward_send, backward_send),
+            (forward_expert, backward_expert),
+            (forward_finish, backward_finish),
+        ):
+            pl.when(runs_behind)(functools.partial(backward_part, bm))
+            pl.when(runs_ahead)(functools.partial(forward_part, fm))
         return carry
 
-    lax.fori_loop(0, micro, forward, 0)
-
-    def backward(m, carry):
-        @pl.when(section < last)
-        def _():
-            pass_on(grad_ref, upg, 1, m, section).wait_recv()
-
-        dy = upg[m]
-        send[2, m] = (first_dims(high_s[m], dy) + first_dims(low_s[m], dy)).astype(bf16)
-        exchange(2, m)
-        arrive(2, m)
-        for at in range(0, hid, tile):
-            cols = pl.ds(at, tile)
-            d_hidden = contract_last(recv[2, m], wd[cols, :])
-            gate = gates[m, :, cols]
-            up = ups[m, :, cols]
-            sig = jax.nn.sigmoid(gate)
-            hid_a[:, cols] = (d_hidden * up * sig * (1.0 + gate * (1.0 - sig))).astype(bf16)
-            hid_b[:, cols] = (d_hidden * gate * sig).astype(bf16)
-        for at in range(0, width, tile):
-            cols = pl.ds(at, tile)
-            send[3, m, :, cols] = (
-                contract_last(hid_a[...], wg[cols, :]) + contract_last(hid_b[...], wu[cols, :])
-            ).astype(bf16)
-        exchange(3, m)
-        arrive(3, m)
-        d_normed = jnp.dot(pick_s[m], recv[3, m], preferred_element_type=f32)
-        values, scale = normed_parts(m)
-        scaled = d_normed * gain
-        inner = jnp.mean(scaled * values, axis=-1, keepdims=True)
-        grad_ref[m] = (
-            upg[m].astype(f32) + scale * scaled - values * scale * scale * scale * inner
-        ).astype(bf16)
-
-        @pl.when(section > 0)
-        def _():
-            pass_on(grad_ref, upg, 1, m, section - 1).start()
-
-        return carry
-
-    lax.fori_loop(0, micro, backward, 0)
+    lax.fori_loop(0, micro + 2 * sections - 1, tick, 0)
 
     def finish(m, carry):
-        for kind in range(4):
-            sent(kind, m)
-
-        @pl.when(section < last)
-        def _():
-            pass_on(out_ref, act, 0, m, section + 1).wait_send()
-
-        @pl.when(section > 0)
-        def _():
-            pass_on(grad_ref, upg, 1, m, section - 1).wait_send()
+        for part in range(parts):
+            for kind in range(4):
+                sent(kind, m, part)
+
+            @pl.when(section < last)
+            def _():
+                pass_on(out_ref, act, 0, m, part, section + 1).wait_send()
+
+            @pl.when(section > 0)
+            def _():
+                pass_on(grad_ref, upg, 1, m, part, section - 1).wait_send()
 
         return carry
 
@@ -521,11 +586,12 @@
             pltpu.VMEM((micro, rows, slots), bf16),
             pltpu.VMEM((slots, hid), bf16),
             pltpu.VMEM((slots, hid), bf16),
+            pltpu.VMEM((slots, hid), f32),
             pltpu.SemaphoreType.DMA((3,)),
-            pltpu.SemaphoreType.DMA((kinds, micro)),
-            pltpu.SemaphoreType.DMA((kinds, micro)),
-            pltpu.SemaphoreType.DMA((2, micro)),
-            pltpu.SemaphoreType.DMA((2, micro)),
+            pltpu.SemaphoreType.DMA((kinds, micro, PARTS)),
+            pltpu.SemaphoreType.DMA((kinds, micro, PARTS)),
+            pltpu.SemaphoreType.DMA((2, micro, PARTS)),
+            pltpu.SemaphoreType.DMA((2, micro, PARTS)),
         ],
         compiler_params=pltpu.CompilerParams(
             collective_id=0, has_side_effects=True, vmem_limit_bytes=56 * 2**20

time: 363 us -> 323 us (0.89)
  Pallas kernels: 355 us -> 316 us
    pallas_call x1, Pallas kernels: 355 us -> 316 us  [shards(): pl.pallas_call(functools.partial(kernel, sections, experts, capacity), ou...]
where the time goes in v2:
time: 323 us
  Pallas kernels  316 us (98%)
  local copies, waits for them, and re-layouts  6.59 us (2%)
    pallas_call x1, Pallas kernels, shards(): pl.pallas_call(functools.partial(kernel, sections, experts, capacity), ou...  316 us
    unnamed x4, local copies, waits for them, and re-layouts  6.59 us

profile of v2, /device:TPU:0, one launch (start us, length us, event | category | flops | bytes accessed | tf_op | source)
XLA Modules:
  0.0 322.8 jit_solution(15194139594560552957)
XLA Ops:
  0.6 1.4 copy.10
  2.0 1.4 copy.11
  3.5 315.6 %shard_map.95 = (bf16[4,32,2048]{2,1,0:T(8,128)(2,1)}, bf16[4,32,2048]{2,1,0:T(8,128)(2,1)}) custom-call(bf16[4,32,2048]{2,1,0:T(8,128)(2,1)} %x_ref.1, bf16[4,32,2048]{2,1,0:T(8,128)(2,1)} %ct_ref.1, bf16[1,2048]{1,0:T(2,128)(2,1)} %gain_ref.1, s32[4,32,2]{2,1,0:T(8,128)} %bitcast.12, f32[4,32,2]{2,1,0:T(8,128)} %bitcast.13, bf16[2048,768]{1,0:T(8,128)(2,1)} %bitcast.7, ...), custom_call_target="tpu_custom_call" | custom-call | tf_op jit(solution)/shard_map/pallas_call | solution.py:566
  319.1 1.9 copy.14
  320.9 1.9 copy.15

commit v3 on v2

--- a/solution.py
+++ b/solution.py
@@ -345,7 +345,7 @@
 
     def exchange(kind, m, part):
         cols = span(part)
-        for off in range(1, experts):
+        for off in sorted(range(1, experts), key=lambda o: -abs(o - experts // 2)):
             peer = lax.rem(me + off, experts)
             pltpu.make_async_remote_copy(
                 src_ref=send.at[kind, m, block(peer), cols],

time: 323 us -> 323 us (level)
  no operation moved by 1% of the time
where the time goes in v3:
time: 323 us; the launch traced here: 322 us
  Pallas kernels  315 us (98%)
  local copies, waits for them, and re-layouts  6.59 us (2%)
    pallas_call x1, Pallas kernels, shards(): pl.pallas_call(functools.partial(kernel, sections, experts, capacity), ou...  315 us
    unnamed x4, local copies, waits for them, and re-layouts  6.59 us

profile of v3, /device:TPU:0, one launch (start us, length us, event | category | flops | bytes accessed | tf_op | source)
XLA Modules:
  0.0 322.4 jit_solution(2472498709051100278)
XLA Ops:
  0.6 1.4 copy.10
  2.0 1.4 copy.11
  3.5 315.2 %shard_map.95 = (bf16[4,32,2048]{2,1,0:T(8,128)(2,1)}, bf16[4,32,2048]{2,1,0:T(8,128)(2,1)}) custom-call(bf16[4,32,2048]{2,1,0:T(8,128)(2,1)} %x_ref.1, bf16[4,32,2048]{2,1,0:T(8,128)(2,1)} %ct_ref.1, bf16[1,2048]{1,0:T(2,128)(2,1)} %gain_ref.1, s32[4,32,2]{2,1,0:T(8,128)} %bitcast.12, f32[4,32,2]{2,1,0:T(8,128)} %bitcast.13, bf16[2048,768]{1,0:T(8,128)(2,1)} %bitcast.7, ...), custom_call_target="tpu_custom_call" | custom-call | tf_op jit(solution)/shard_map/pallas_call | solution.py:566
  318.7 1.9 copy.14
  320.5 1.9 copy.15
